TPU v7x, 1024 devices: a whole 8x8x8 slice. The times are simulated.
1024 devices in a mesh: dp: 16 (over z, core), expert: 64 (over x, y).
Axes of the slice: x: 8, y: 8, z: 8, core: 2. Of those that a mesh axis runs over, the one named last changes fastest.
Arguments:
- grad_out: bfloat16 [131072, 1024], P(('dp', 'expert')), may hold values from -6 to 6
- routes: int32 [131072, 2], P(('dp', 'expert')), may hold values from 0 to 255, all different within a row; in each aligned block of 128 rows (0 to 127, 128 to 255, ...) at most 2 rows name the same one
- gates: float32 [131072, 2], P(('dp', 'expert')), may hold values from 0.2 to 1
- weights: bfloat16 [64, 3584, 1024], P('expert'), may hold values from -0.1875 to 0.1875
- saved_inputs: bfloat16 [16, 64, 128, 3584], P('dp', 'expert'), may hold values from -0.29882812 to 0.29882812
Outputs:
- input_grad: bfloat16 [131072, 3584], P(('dp', 'expert'))
- weight_grad: bfloat16 [64, 3584, 1024], P('expert', 'dp')
Inputs may be any that keep to these rules, and one draw needn't show every extreme that they name: `routes`: each row names 2 different experts. Expert e < 64 is held on index e of expert. Among the tokens of one device no expert is named more than 2 times. Entries of saved_inputs whose slot is empty are never read.
All inputs are finite; a program needn't handle non-finite values.
Results may differ from a plain program's by a relative error of at most 0.025.
Values may be sent and summed in bfloat16 or wider, within the bound.
A program may use at most 64 MiB of HBM per device.

v0:
```python
import jax
import jax.numpy as jnp
from jax import lax
from jax.sharding import PartitionSpec as P


def on_device(grad_out, routes, gates, weights, saved_inputs):
    experts = lax.axis_size("expert")
    replicas_count = lax.axis_size("dp")
    tok_rows = grad_out.shape[0]
    pick_count = routes.shape[1]
    slots_all = saved_inputs.shape[2]
    capacity = slots_all // experts
    model_width = saved_inputs.shape[3]
    band_rows = model_width // replicas_count
    slot_ids = routes.reshape(-1)
    slot_gate = gates.reshape(-1)
    onehot = (slot_ids[:, None] == jnp.arange(experts, dtype=jnp.int32)[None, :]).astype(jnp.int32)
    ranking = jnp.cumsum(onehot, axis=0) - onehot
    placed = jnp.sum(ranking * onehot, axis=1)
    inside = jnp.sum(onehot, axis=1)
    target = jnp.where(inside > 0, slot_ids * capacity + placed, slots_all)
    place_table = target[None, :] == jnp.arange(slots_all, dtype=jnp.int32)[:, None]
    token_table = jnp.sum(
        place_table.reshape(slots_all, tok_rows, pick_count).astype(jnp.int32), axis=2
    ).astype(jnp.bfloat16)
    send_rows = jnp.dot(token_table, grad_out, preferred_element_type=jnp.float32).astype(
        jnp.bfloat16
    )
    send_rows = send_rows.reshape(experts, capacity, -1)
    send_gates = jnp.sum(jnp.where(place_table, slot_gate[None, :], 0.0), axis=1).reshape(
        experts, capacity
    )
    weight = weights[0]
    expert_rows = lax.all_to_all(send_rows, "expert", split_axis=0, concat_axis=0, tiled=True)
    row_gates = lax.all_to_all(
        send_gates.astype(jnp.bfloat16), "expert", split_axis=0, concat_axis=0, tiled=True
    ).astype(send_gates.dtype)
    answers = lax.dot_general(
        expert_rows, weight, (((2,), (1,)), ((), ())), preferred_element_type=jnp.float32
    ).astype(jnp.bfloat16)
    scaled = (row_gates[:, :, None] * expert_rows.astype(jnp.float32)).astype(jnp.bfloat16)
    returned = lax.all_to_all(answers, "expert", split_axis=0, concat_axis=0, tiled=True)
    returned, scaled = (returned, scaled)
    saved_rows = saved_inputs.reshape(slots_all, model_width)
    scaled_rows = scaled.reshape(slots_all, -1)
    summed_grad = lax.psum_scatter(
        lax.dot_general(
            saved_rows, scaled_rows, (((0,), (0,)), ((), ())), preferred_element_type=jnp.float32
        ).astype(jnp.bfloat16),
        "dp",
        scatter_dimension=0,
        tiled=True,
    )
    weight_grad = summed_grad.reshape(1, band_rows, -1)
    flat_back = returned.reshape(slots_all, model_width)
    clipped = jnp.minimum(target, slots_all - 1)
    picked = jnp.take(flat_back, clipped, axis=0)
    weight_slot = jnp.where(inside > 0, slot_gate, 0.0)
    combined = jnp.sum(
        picked.reshape(tok_rows, pick_count, model_width).astype(jnp.float32)
        * weight_slot.reshape(tok_rows, pick_count, 1),
        axis=1,
    )
    return (combined.astype(jnp.bfloat16), weight_grad)


def solution(mesh):
    return jax.shard_map(
        on_device,
        mesh=mesh,
        in_specs=(
            P(("dp", "expert"), None),
            P(("dp", "expert"), None),
            P(("dp", "expert"), None),
            P("expert", None, None),
            P("dp", "expert", None, None),
        ),
        out_specs=(P(("dp", "expert"), None), P("expert", "dp", None)),
        check_vma=False,
    )
```

profile of v0, /device:TPU:1, one launch (start us, length us, event | category | flops | bytes accessed | tf_op | source)
XLA Modules:
  0.0 156.3 jit_solution(4314435769297972511)
XLA Ops:
  7.2 0.9 copy.49
  8.3 0.8 copy.58
  9.3 0.6 reduce-window.6
  10.3 0.8 convert_element_type.77
  11.1 14.0 %all-to-all-start.2 = ((bf16[64,1,2]{2,1,0:T(2,128)(2,1)}), bf16[64,1,2]{2,1,0:T(2,128)(2,1)S(1)}, u32[]{:S(2)}, u32[]{:S(2)}) async-start(bf16[64,1,2]{2,1,0:T(2,128)(2,1)} %convert_element_type.77), calls=%async_computation.2 | async-start | bytes 65536 | tf_op jit(solution)/shard_map/all_to_all | solution.py:36
  25.6 0.7 compare_and_fusion
  26.4 1.2 convolution_convert_fusion.1
  27.6 0.8 reshape.152
  28.4 7.6 %all-to-all-done.2 = bf16[64,1,2]{2,1,0:T(2,128)(2,1)S(1)} async-done(((bf16[64,1,2]{2,1,0:T(2,128)(2,1)}), bf16[64,1,2]{2,1,0:T(2,128)(2,1)S(1)}, u32[]{:S(2)}, u32[]{:S(2)}) %all-to-all-start.2) | async-done | bytes 288 | tf_op jit(solution)/shard_map/all_to_all | solution.py:36
  36.0 4.6 %all-to-all-start = ((bf16[64,2,1024]{2,1,0:T(2,128)(2,1)}), bf16[64,2,1024]{2,1,0:T(2,128)(2,1)S(1)}, u32[]{:S(2)}, u32[]{:S(2)}) async-start(bf16[64,2,1024]{2,1,0:T(2,128)(2,1)} %reshape.152), calls=%async_computation | async-start | bytes 524288 | tf_op jit(solution)/shard_map/all_to_all | solution.py:35
  40.8 12.3 %all-to-all-done = bf16[64,2,1024]{2,1,0:T(2,128)(2,1)S(1)} async-done(((bf16[64,2,1024]{2,1,0:T(2,128)(2,1)}), bf16[64,2,1024]{2,1,0:T(2,128)(2,1)S(1)}, u32[]{:S(2)}, u32[]{:S(2)}) %all-to-all-start) | async-done | bytes 262176 | tf_op jit(solution)/shard_map/all_to_all | solution.py:35
  53.6 5.1 %fusion.2 = bf16[3584,1024]{0,1:T(8,128)(2,1)} fusion(bf16[128,1024]{1,0:T(8,128)(2,1)S(1)} %reshape.154, bf16[1,1,128,3584]{3,2,1,0:T(8,128)(2,1)S(1)} %copy-done), kind=kOutput, calls=%fused_computation.4 | convolution fusion | flops 943194112 | bytes 8519680 | tf_op jit(solution)/shard_map/dot_general | solution.py:48
  58.7 10.4 %copy.64 = bf16[3584,1024]{1,0:T(8,128)(2,1)} copy(bf16[3584,1024]{0,1:T(8,128)(2,1)} %fusion.2) | data formatting | bytes 14680064
  69.1 5.6 %fusion.3 = bf16[64,2,3584]{2,0,1:T(8,128)(2,1)S(1)} fusion(bf16[1,3584,1024]{2,1,0:T(8,128)(2,1)} %param.8, bf16[64,2,1024]{2,1,0:T(2,128)(2,1)S(1)} %all-to-all-done), kind=kOutput, calls=%fused_computation.5 | convolution fusion | flops 939982848 | bytes 8519680 | tf_op jit(solution)/shard_map/dot_general | solution.py:39
  74.7 1.9 %copy.56 = bf16[64,2,3584]{2,1,0:T(2,128)(2,1)} copy(bf16[64,2,3584]{2,0,1:T(8,128)(2,1)S(1)} %fusion.3) | data formatting | bytes 1835008 | tf_op jit(solution)/shard_map/convert_element_type | solution.py:41
  76.6 4.8 %all-to-all-start.1 = ((bf16[64,2,3584]{2,1,0:T(2,128)(2,1)}), bf16[64,2,3584]{2,1,0:T(2,128)(2,1)S(1)}, u32[]{:S(2)}, u32[]{:S(2)}) async-start(bf16[64,2,3584]{2,1,0:T(2,128)(2,1)} %copy.56), calls=%async_computation.1 | async-start | bytes 1835008 | tf_op jit(solution)/shard_map/all_to_all | solution.py:43
  81.9 17.8 %all-to-all-done.1 = bf16[64,2,3584]{2,1,0:T(2,128)(2,1)S(1)} async-done(((bf16[64,2,3584]{2,1,0:T(2,128)(2,1)}), bf16[64,2,3584]{2,1,0:T(2,128)(2,1)S(1)}, u32[]{:S(2)}, u32[]{:S(2)}) %all-to-all-start.1) | async-done | bytes 917536 | tf_op jit(solution)/shard_map/all_to_all | solution.py:43
  99.7 0.3 reshape.153
  100.1 3.1 %gather_fusion = bf16[256,3584]{1,0:T(8,128)(2,1)} fusion(bf16[128,3584]{1,0:T(8,128)(2,1)S(1)} %reshape.153, s32[1024]{0:T(1024)S(1)} %pad_clamp_fusion), kind=kCustom, calls=%fused_computation | custom fusion | bytes 3671040 | tf_op jit(solution)/shard_map/jit(_take)/gather | solution.py:58
  103.1 3.9 %gather.7 = bf16[128,2,3584]{2,1,0:T(2,128)(2,1)S(1)} reshape(bf16[256,3584]{1,0:T(8,128)(2,1)} %gather_fusion) | data formatting | bytes 3670016 | tf_op jit(solution)/shard_map/jit(_take)/gather | solution.py:58
  107.0 8.5 %multiply_reduce_fusion = bf16[128,3584]{1,0:T(8,128)(2,1)} fusion(bf16[128,2,3584]{2,1,0:T(2,128)(2,1)S(1)} %gather.7, pred[128,2]{1,0:T(8,128)(4,1)S(1)} %copy.54, f32[128,2]{1,0:T(8,128)S(1)} %broadcast_select_fusion.1), kind=kLoop, calls=%fused_computation.6 | loop fusion | flops 3211264 | bytes 2753792 | tf_op jit(solution)/shard_map/reduce_sum | solution.py:60
  115.5 31.8 %reduce-scatter.4.cloned.1.call-done = bf16[224,1024]{1,0:T(8,128)(2,1)} async-done(((bf16[3584,1024]{1,0:T(8,128)(2,1)}), bf16[224,1024]{1,0:T(8,128)(2,1)}) %reduce-scatter.4.cloned.1.call-update) | async-done | bytes 458768
  147.3 1.2 copy.65
  148.5 1.0 copy.63
  (33 shorter events, 2.4 us)
Async XLA Ops:
  7.2 46.4 %copy-start = (bf16[1,1,128,3584]{3,2,1,0:T(8,128)(2,1)S(1)}, bf16[1,1,128,3584]{3,2,1,0:T(8,128)(2,1)}, u32[]{:S(2)}) copy-start(bf16[1,1,128,3584]{3,2,1,0:T(8,128)(2,1)} %param.9) | copy-start | bytes 2752516
  11.1 24.8 %all-to-all-start.2 = ((bf16[64,1,2]{2,1,0:T(2,128)(2,1)}), bf16[64,1,2]{2,1,0:T(2,128)(2,1)S(1)}, u32[]{:S(2)}, u32[]{:S(2)}) async-start(bf16[64,1,2]{2,1,0:T(2,128)(2,1)} %convert_element_type.77), calls=%async_computation.2 | async-start | bytes 65536 | tf_op jit(solution)/shard_map/all_to_all | solution.py:36
  36.0 17.2 %all-to-all-start = ((bf16[64,2,1024]{2,1,0:T(2,128)(2,1)}), bf16[64,2,1024]{2,1,0:T(2,128)(2,1)S(1)}, u32[]{:S(2)}, u32[]{:S(2)}) async-start(bf16[64,2,1024]{2,1,0:T(2,128)(2,1)} %reshape.152), calls=%async_computation | async-start | bytes 524288 | tf_op jit(solution)/shard_map/all_to_all | solution.py:35
  40.6 106.7 %reduce-scatter.4.cloned.1.call-start = ((), (), s32[]{:S(2)}) async-start(), calls=%async_computation.4 | async-start | bytes 7798784
  74.7 6.7 %copy-start.1 = (s32[128,2]{0,1:T(2,128)S(1)}, s32[128,2]{0,1:T(2,128)}, u32[]{:S(2)}) copy-start(s32[128,2]{0,1:T(2,128)} %param.6) | copy-start | bytes 3076
  76.6 23.1 %all-to-all-start.1 = ((bf16[64,2,3584]{2,1,0:T(2,128)(2,1)}), bf16[64,2,3584]{2,1,0:T(2,128)(2,1)S(1)}, u32[]{:S(2)}, u32[]{:S(2)}) async-start(bf16[64,2,3584]{2,1,0:T(2,128)(2,1)} %copy.56), calls=%async_computation.1 | async-start | bytes 1835008 | tf_op jit(solution)/shard_map/all_to_all | solution.py:43
Sparse Core Ops, SparseCore 0:
  69.2 78.0 reduce-scatter.3
where the time goes:
time: 159 us; the launch traced here: 156 us
  waiting for transfers between devices  69.5 us (44%)
  local copies, waits for them, and re-layouts  26.7 us (17%)
  starting transfers between devices  23.5 us (15%)
  between operations  14.2 us (9%)
  matrix products  11.9 us (7%)
  other arithmetic  10.4 us (7%)
    unnamed x2, waiting for transfers between devices  31.8 us
    all_to_all x1, waiting for transfers between devices, on_device(): lax.all_to_all(answers, 'expert', split_axis=0, concat_axis=0, tiled=True)  17.8 us
    unnamed x9, local copies, waits for them, and re-layouts  14.3 us
    all_to_all x1, starting transfers between devices, on_device(): lax.all_to_all(send_gates.astype(jnp.bfloat16), 'expert', split_axis=0, c...  14 us
    all_to_all x1, waiting for transfers between devices, on_device(): lax.all_to_all(send_rows, 'expert', split_axis=0, concat_axis=0, tiled=True)  12.3 us
    reduce_sum x1, other arithmetic, on_device(): jnp.sum(picked.reshape(tok_rows, pick_count, model_width).astype(jnp.floa...  8.51 us
    all_to_all x1, waiting for transfers between devices, on_device(): lax.all_to_all(send_gates.astype(jnp.bfloat16), 'expert', split_axis=0, c...  7.6 us
    gather x2, local copies, waits for them, and re-layouts, on_device(): picked = jnp.take(flat_back, clipped, axis=0)  6.94 us
  transfers between devices with their start and end apart: 4, of which 4 were waited for; matrix products, arithmetic and copies ran while one was open for 17% of the time, Pallas kernels for 0%

commit v1 on v0

v1 whole, which is shorter than its diff:
```python
import jax
import jax.numpy as jnp
from jax import lax
from jax.sharding import PartitionSpec as P


def on_device(grad_out, routes, gates, weights, saved_inputs):
    experts = lax.axis_size("expert")
    tok_rows, ff = grad_out.shape
    slots_all = saved_inputs.shape[2]
    capacity = slots_all // experts
    model_width = saved_inputs.shape[3]
    saved_rows = saved_inputs.reshape(slots_all, model_width)
    saved_band = lax.all_to_all(saved_rows, "dp", split_axis=1, concat_axis=0, tiled=True)

    ids, gate_rows = routes.T, gates.T
    slot = lax.broadcasted_iota(jnp.int32, (slots_all, tok_rows), 0)
    slot_expert, slot_rank = slot // capacity, slot % capacity
    hits = [slot_expert == ids[k][None, :] for k in range(ids.shape[0])]
    named = (hits[0] | hits[1]).astype(jnp.bfloat16)
    row = lax.broadcasted_iota(jnp.int32, (tok_rows, tok_rows), 0)
    column = lax.broadcasted_iota(jnp.int32, (tok_rows, tok_rows), 1)
    earlier = jnp.dot(named, (row < column).astype(jnp.bfloat16), preferred_element_type=jnp.float32)
    filled = (hits[0] | hits[1]) & (earlier == slot_rank.astype(jnp.float32))
    gate = jnp.where(hits[0], gate_rows[0][None, :], gate_rows[1][None, :])
    slot_gate = jnp.sum(jnp.where(filled, gate, 0.0), axis=1, keepdims=True)
    table = filled.astype(jnp.bfloat16)

    picked = jnp.dot(table, grad_out, preferred_element_type=jnp.float32)
    scaled_out = (picked * slot_gate).astype(jnp.bfloat16)
    scaled = lax.all_to_all(
        scaled_out.reshape(experts, capacity, ff), "expert", split_axis=0, concat_axis=0, tiled=True
    ).reshape(slots_all, ff)

    scaled_all = lax.all_gather(scaled, "dp", axis=0, tiled=True)
    answers = lax.dot_general(
        scaled, weights[0], (((1,), (1,)), ((), ())), preferred_element_type=jnp.float32
    ).astype(jnp.bfloat16)
    returned = lax.all_to_all(
        answers.reshape(experts, capacity, model_width), "expert", split_axis=0, concat_axis=0, tiled=True
    ).reshape(slots_all, model_width)
    input_grad = lax.dot_general(
        table, returned, (((0,), (0,)), ((), ())), preferred_element_type=jnp.float32
    ).astype(jnp.bfloat16)
    weight_grad = lax.dot_general(
        saved_band, scaled_all, (((0,), (0,)), ((), ())), preferred_element_type=jnp.float32
    ).astype(jnp.bfloat16)
    return input_grad, weight_grad[None]


def solution(mesh):
    return jax.shard_map(
        on_device,
        mesh=mesh,
        in_specs=(
            P(("dp", "expert"), None),
            P(("dp", "expert"), None),
            P(("dp", "expert"), None),
            P("expert", None, None),
            P("dp", "expert", None, None),
        ),
        out_specs=(P(("dp", "expert"), None), P("expert", "dp", None)),
        check_vma=False,
    )
```

time: 159 us -> 131 us (0.82); the launches traced: 156 us -> 130 us
  waiting for transfers between devices: 69.5 us -> 42.3 us
  blocking collectives: 0 us -> 26.3 us
  local copies, waits for them, and re-layouts: 26.7 us -> 5.35 us
  other arithmetic: 10.4 us -> 0.02 us
  starting transfers between devices: 23.5 us -> 30.6 us
    unnamed x2 -> x1, waiting for transfers between devices: 31.8 us -> 0.02 us
    all_to_all x0 -> x1, blocking collectives: none -> 26.3 us  [on_device(): lax.all_to_all(scaled_out.reshape(experts, capacity, ff), 'expert', split...]
    unnamed x9 -> x5, local copies, waits for them, and re-layouts: 14.3 us -> 1.32 us
    reduce_sum x4 -> x0, other arithmetic: 8.75 us -> none  [the longest x1 8.51 us: on_device(): jnp.sum(picked.reshape(tok_rows, pick_count, model_width).astype(jnp.floa...]
    all_to_all x3 -> x2, starting transfers between devices: 23.5 us -> 30.6 us  [the longest x1 25.9 us: on_device(): lax.all_to_all(saved_rows, 'dp', split_axis=1, concat_axis=0, tiled=True)]
    gather x2 -> x0, local copies, waits for them, and re-layouts: 6.94 us -> none  [on_device(): picked = jnp.take(flat_back, clipped, axis=0)]
    all_to_all x3 -> x2, waiting for transfers between devices: 37.7 us -> 42.3 us  [the longest x1 23.6 us: on_device(): lax.all_to_all(saved_rows, 'dp', split_axis=1, concat_axis=0, tiled=True)]
    convert_element_type x3 -> x0, local copies, waits for them, and re-layouts: 2.76 us -> none  [the longest x1 1.87 us: on_device(): answers = lax.dot_general(expert_rows, weight, (((2,), (1,)), ((), ())),...]
  transfers between devices with their start and end apart: 4 -> 3, of which waited for: 4 -> 2; matrix products, arithmetic and copies ran while one was open for 17% -> 8% of each run, Pallas kernels for 0% -> 0%
where the time goes in v1:
time: 131 us; the launch traced here: 130 us
  waiting for transfers between devices  42.3 us (32%)
  starting transfers between devices  30.6 us (23%)
  blocking collectives  26.3 us (20%)
  between operations  14.1 us (11%)
  matrix products  11.7 us (9%)
  local copies, waits for them, and re-layouts  5.35 us (4%)
    all_to_all x1, blocking collectives, on_device(): lax.all_to_all(scaled_out.reshape(experts, capacity, ff), 'expert', split...  26.3 us
    all_to_all x1, starting transfers between devices, on_device(): lax.all_to_all(saved_rows, 'dp', split_axis=1, concat_axis=0, tiled=True)  25.9 us
    all_to_all x1, waiting for transfers between devices, on_device(): lax.all_to_all(saved_rows, 'dp', split_axis=1, concat_axis=0, tiled=True)  23.6 us
    all_to_all x1, waiting for transfers between devices, on_device(): lax.all_to_all(answers.reshape(experts, capacity, model_width), 'expert',...  18.6 us
    dot_general x1, matrix products, on_device(): lax.dot_general(scaled, weights[0], (((1,), (1,)), ((), ())), preferred_e...  5.77 us
    all_to_all x1, starting transfers between devices, on_device(): lax.all_to_all(answers.reshape(experts, capacity, model_width), 'expert',...  4.65 us
    dot_general x1, matrix products, on_device(): lax.dot_general(saved_band, scaled_all, (((0,), (0,)), ((), ())), preferr...  4.07 us
  transfers between devices with their start and end apart: 3, of which 2 were waited for; matrix products, arithmetic and copies ran while one was open for 8% of the time, Pallas kernels for 0%

profile of v1, /device:TPU:1, one launch (start us, length us, event | category | flops | bytes accessed | tf_op | source)
XLA Modules:
  0.0 130.4 jit_solution(642270686490083594)
XLA Ops:
  7.2 0.0 copy-start
  7.2 0.0 all-gather.2.cloned.1.call-start
  7.3 0.8 slice_bitcast_fusion.3
  8.0 0.8 slice_bitcast_fusion.1
  8.8 0.3 fusion.13
  9.1 0.0 copy-done
  9.1 0.3 fusion.6
  9.3 0.1 reshape.22
  9.4 26.3 %all_to_all.29 = bf16[64,2,1024]{2,1,0:T(2,128)(2,1)S(1)} all-to-all(bf16[64,2,1024]{2,1,0:T(2,128)(2,1)S(1)} %reshape.22), channel_id=1, replica_groups=mesh['dp'=16,'expert'=64] {'expert'}, dimensions={0} | all-to-all | bytes 524288 | tf_op jit(solution)/shard_map/all_to_all | solution.py:31
  35.8 0.8 reshape.23
  36.6 0.0 all-gather.2.cloned.1.call-update
  36.6 0.0 copy-start.1
  36.6 5.8 %fusion.2 = bf16[128,3584]{1,0:T(8,128)(2,1)S(1)} fusion(bf16[128,1024]{1,0:T(8,128)(2,1)} %reshape.23, bf16[1,3584,1024]{2,1,0:T(8,128)(2,1)} %param.8), kind=kOutput, calls=%fused_computation.2 | convolution fusion | flops 939982848 | bytes 8519680 | tf_op jit(solution)/shard_map/dot_general | solution.py:36
  42.4 1.3 reshape.24
  43.6 4.6 %all-to-all-start.1 = ((bf16[64,2,3584]{2,1,0:T(2,128)(2,1)}), bf16[64,2,3584]{2,1,0:T(2,128)(2,1)S(1)}, u32[]{:S(2)}, u32[]{:S(2)}) async-start(bf16[64,2,3584]{2,1,0:T(2,128)(2,1)} %reshape.24), calls=%async_computation.1 | async-start | bytes 1835008 | tf_op jit(solution)/shard_map/all_to_all | solution.py:39
  48.3 0.0 copy-done.1
  48.3 1.3 copy.7
  49.6 18.6 %all-to-all-done.1 = bf16[64,2,3584]{2,1,0:T(2,128)(2,1)S(1)} async-done(((bf16[64,2,3584]{2,1,0:T(2,128)(2,1)}), bf16[64,2,3584]{2,1,0:T(2,128)(2,1)S(1)}, u32[]{:S(2)}, u32[]{:S(2)}) %all-to-all-start.1) | async-done | bytes 917536 | tf_op jit(solution)/shard_map/all_to_all | solution.py:39
  68.2 25.9 %all-to-all-start.2 = ((bf16[128,16,224]{0,2,1:T(8,128)(2,1)}), bf16[128,16,224]{0,2,1:T(8,128)(2,1)S(1)}, u32[]{:S(2)}, u32[]{:S(2)}) async-start(bf16[128,16,224]{0,2,1:T(8,128)(2,1)} %bitcast.7), calls=%async_computation.2 | async-start | bytes 1835008 | tf_op jit(solution)/shard_map/all_to_all | solution.py:14
  94.2 0.3 reshape.25
  94.5 1.3 %convolution_convert_fusion = bf16[128,3584]{1,0:T(8,128)(2,1)} fusion(pred[128,128]{0,1:T(32,128)(4,1)S(1)} %get-tuple-element.7, bf16[128,3584]{1,0:T(8,128)(2,1)S(1)} %reshape.25), kind=kOutput, calls=%fused_computation.3 | convolution fusion | flops 117899264 | bytes 1851392 | tf_op jit(solution)/shard_map/dot_general | solution.py:42
  95.8 23.6 %all-to-all-done.2 = bf16[128,16,224]{0,2,1:T(8,128)(2,1)S(1)} async-done(((bf16[128,16,224]{0,2,1:T(8,128)(2,1)}), bf16[128,16,224]{0,2,1:T(8,128)(2,1)S(1)}, u32[]{:S(2)}, u32[]{:S(2)}) %all-to-all-start.2) | async-done | bytes 917536 | tf_op jit(solution)/shard_map/all_to_all | solution.py:14
  119.5 0.0 all-gather.2.cloned.1.call-done
  119.5 4.1 %fusion.5 = bf16[1,224,1024]{2,1,0:T(8,128)(2,1)} fusion(bf16[2048,1024]{1,0:T(8,128)(2,1)} %all-gather.2.cloned.1.call-done, bf16[128,16,224]{0,2,1:T(8,128)(2,1)S(1)} %all-to-all-done.2), kind=kOutput, calls=%fused_computation.6 | convolution fusion | flops 939753472 | bytes 5570560 | tf_op jit(solution)/shard_map/dot_general | solution.py:45
  (3 shorter events, 0.0 us)
Async XLA Ops:
  7.2 1.9 %copy-start = (bf16[128,1024]{1,0:T(8,128)(2,1)S(1)}, bf16[128,1024]{1,0:T(8,128)(2,1)}, u32[]{:S(2)}) copy-start(bf16[128,1024]{1,0:T(8,128)(2,1)} %param.5) | copy-start | bytes 786436
  7.2 112.3 %all-gather.2.cloned.1.call-start = ((), (), s32[]{:S(2)}) async-start(), calls=%async_computation.3 | async-start | bytes 4456448 | tf_op jit(solution)/shard_map/all_gather | solution.py:35
  36.6 11.7 %copy-start.1 = (bf16[1,1,128,3584]{3,2,1,0:T(8,128)(2,1)S(1)}, bf16[1,1,128,3584]{3,2,1,0:T(8,128)(2,1)}, u32[]{:S(2)}) copy-start(bf16[1,1,128,3584]{3,2,1,0:T(8,128)(2,1)} %param.9) | copy-start | bytes 2752516
  43.6 24.6 %all-to-all-start.1 = ((bf16[64,2,3584]{2,1,0:T(2,128)(2,1)}), bf16[64,2,3584]{2,1,0:T(2,128)(2,1)S(1)}, u32[]{:S(2)}, u32[]{:S(2)}) async-start(bf16[64,2,3584]{2,1,0:T(2,128)(2,1)} %reshape.24), calls=%async_computation.1 | async-start | bytes 1835008 | tf_op jit(solution)/shard_map/all_to_all | solution.py:39
  68.2 51.2 %all-to-all-start.2 = ((bf16[128,16,224]{0,2,1:T(8,128)(2,1)}), bf16[128,16,224]{0,2,1:T(8,128)(2,1)S(1)}, u32[]{:S(2)}, u32[]{:S(2)}) async-start(bf16[128,16,224]{0,2,1:T(8,128)(2,1)} %bitcast.7), calls=%async_computation.2 | async-start | bytes 1835008 | tf_op jit(solution)/shard_map/all_to_all | solution.py:14
Sparse Core Ops, SparseCore 0:
  36.7 54.6 all-gather.1

commit v2 on v1

v2 whole, which is shorter than its diff:
```python
import functools

import jax
import jax.numpy as jnp
from jax import lax
from jax.experimental import pallas as pl
from jax.experimental.pallas import tpu as pltpu
from jax.sharding import PartitionSpec as P

MESH = pl.DeviceIdType.MESH
BF16, F32 = jnp.bfloat16, jnp.float32


def nn(a, b):
    return jnp.dot(a, b, preferred_element_type=F32)


def nt(a, b):
    return lax.dot_general(a, b, (((1,), (1,)), ((), ())), preferred_element_type=F32)


def kernel(
    side, chips,
    ids_hbm, gates_hbm, grad_hbm, w_hbm, saved_hbm,
    input_grad, weight_grad,
    ids, gates, grad, w, saved, local_sems,
    rows_out1, rows_in1, rows_out2, rows_in2, rows_sems,
    saved_t, bands, band_sems,
    scaled_all, ring_send, ring_recv, sib_send, sib_recv,
    back_out1, back_in1, back_out2, back_in2, back_sems,
    total,
):
    slots, width = saved.shape
    ff = grad.shape[1]
    half = ff // 2
    part = width // 4
    block = slots // side
    band = bands.shape[1]
    bits = side.bit_length() - 1
    rounds = chips // 2
    rep, spot = lax.axis_index("dp"), lax.axis_index("expert")
    mz, core = lax.div(rep, 2), lax.rem(rep, 2)
    mx, my = lax.div(spot, side), lax.rem(spot, side)

    def along_x(k):
        return {"expert": lax.rem(mx + k, side) * side + my}

    def along_y(k):
        return {"expert": mx * side + lax.rem(my + k, side)}

    def chip_at(k):
        return lax.rem(mz + k + chips, chips)

    barrier = pltpu.get_barrier_semaphore()
    for k in range(1, side):
        pl.semaphore_signal(barrier, inc=1, device_id=along_x(k), device_id_type=MESH)
        pl.semaphore_signal(barrier, inc=1, device_id=along_y(k), device_id_type=MESH)
    for k in range(1, 2 * chips):
        pl.semaphore_signal(
            barrier, inc=1, device_id={"dp": lax.rem(rep + k, 2 * chips)}, device_id_type=MESH
        )

    loads = [
        pltpu.make_async_copy(source, target, local_sems.at[i])
        for i, (source, target) in enumerate(
            ((ids_hbm, ids), (gates_hbm, gates), (grad_hbm, grad), (saved_hbm, saved), (w_hbm, w))
        )
    ]
    for load in loads:
        load.start()

    row = lax.broadcasted_iota(jnp.int32, (slots, slots), 0)
    column = lax.broadcasted_iota(jnp.int32, (slots, slots), 1)
    pair = row >> 1
    swapped = ((pair & (side - 1)) << bits) | (pair >> bits)
    swap = (column == ((swapped << 1) | (row & 1))).astype(F32).astype(BF16)
    same = (row == column).astype(F32).astype(BF16)

    tokens = grad.shape[0]
    slot = lax.broadcasted_iota(jnp.int32, (slots, tokens), 0)
    token_row = lax.broadcasted_iota(jnp.int32, (tokens, tokens), 0)
    token_column = lax.broadcasted_iota(jnp.int32, (tokens, tokens), 1)
    before = (token_row < token_column).astype(F32).astype(BF16)
    eye = (token_row == token_column).astype(F32).astype(BF16)
    for load in loads[:2]:
        load.wait()

    def table_of(expert):
        first, second = expert == ids[0:1, :], expert == ids[1:2, :]
        named = (first | second).astype(F32)
        earlier = nn(named.astype(BF16), before)
        rank = (slot & 1).astype(F32)
        table = jnp.where(earlier == rank, named, 0.0)
        gate = jnp.where(first, gates[0:1, :], jnp.where(second, gates[1:2, :], 0.0))
        slot_gate = jnp.sum(table * gate, axis=1, keepdims=True)
        return table.astype(BF16), slot_gate

    expert = slot >> 1
    table_xy, gate_xy = table_of(expert)
    table_yx, gate_yx = table_of(((expert & (side - 1)) << bits) | (expert >> bits))
    loads[2].wait()
    rows_out1[0] = (nn(table_xy, grad[:, :half]) * gate_xy).astype(BF16)
    rows_out1[1] = (nn(table_yx, grad[:, half:]) * gate_yx).astype(BF16)

    pl.semaphore_wait(barrier, 2 * (side - 1) + 2 * chips - 1)

    def spread(out, into, sems, to_x):
        me, where = (mx, along_x) if to_x else (my, along_y)
        for k in range(1, side):
            there = lax.rem(me + k, side)
            pltpu.make_async_remote_copy(
                src_ref=out.at[pl.ds(pl.multiple_of(there * block, block), block), :],
                dst_ref=into.at[pl.ds(pl.multiple_of(me * block, block), block), :],
                send_sem=sems.at[0],
                recv_sem=sems.at[1],
                device_id=where(k),
                device_id_type=MESH,
            ).start()
        own = pl.ds(pl.multiple_of(me * block, block), block)
        into[own, :] = out[own, :]

    def spread_wait(out, into, sems):
        rest = pl.ds(0, slots - block)
        return pltpu.make_async_remote_copy(
            src_ref=out.at[rest, :],
            dst_ref=into.at[rest, :],
            send_sem=sems.at[0],
            recv_sem=sems.at[1],
            device_id=along_x(1),
            device_id_type=MESH,
        )

    def rows(hop, i):
        out, into = ((rows_out1, rows_in1), (rows_out2, rows_in2))[hop]
        return out.at[i], into.at[i], rows_sems.at[2 * hop + i]

    for i in range(2):
        spread(*rows(0, i), to_x=i == 0)

    loads[3].wait()
    for start in range(0, width, slots):
        saved_t[pl.ds(start, slots), :] = nt(same, saved[:, start : start + slots]).astype(BF16)

    def send_bands(first, last):
        for k in range(first, last):
            for other in range(2):
                if k == 0 and other == 0:
                    continue
                there = chip_at(k) * 2 + lax.rem(core + other, 2)
                pltpu.make_async_remote_copy(
                    src_ref=saved_t.at[pl.ds(pl.multiple_of(there * band, band), band), :],
                    dst_ref=bands.at[mz, :, pl.ds(pl.multiple_of(core * slots, slots), slots)],
                    send_sem=band_sems.at[0, other if k else 2],
                    recv_sem=band_sems.at[1, other if k else 2],
                    device_id={"dp": there},
                    device_id_type=MESH,
                ).start()

    def band_wait(j):
        count = 1 if j == 2 else chips - 1
        some = bands.at[pl.ds(0, count), :, pl.ds(0, slots)]
        return pltpu.make_async_remote_copy(
            src_ref=some,
            dst_ref=some,
            send_sem=band_sems.at[0, j],
            recv_sem=band_sems.at[1, j],
            device_id={"dp": lax.rem(rep + 1, 2 * chips)},
            device_id_type=MESH,
        )

    EARLY(send_bands, chips, 0)
    bands[mz, :, pl.ds(pl.multiple_of(core * slots, slots), slots)] = saved_t[
        pl.ds(pl.multiple_of(rep * band, band), band), :
    ]

    for i in range(2):
        spread_wait(*rows(0, i)).wait_recv()
        rows_out2[i] = nn(swap, rows_in1[i]).astype(BF16)
        spread(*rows(1, i), to_x=i == 1)
    EARLY(send_bands, chips, 1)
    own_rows = pl.ds(pl.multiple_of(rep * slots, slots), slots)
    for i in range(2):
        spread_wait(*rows(1, i)).wait_recv()
    scaled_all[own_rows, pl.ds(0, half)] = nn(swap, rows_in2[0]).astype(BF16)
    scaled_all[own_rows, pl.ds(half, half)] = rows_in2[1]

    def piece(chip, which, h):
        return scaled_all.at[
            pl.ds(pl.multiple_of((chip * 2 + which) * slots, slots), slots), pl.ds(h * half, half)
        ]

    def hops(r):
        return [(0, 0), (1, 0), (0, 1), (1, 1)] if r < rounds else [(0, 0), (1, 1)]

    def ring(r, way, h):
        sign = 1 if way == 0 else -1
        ref = piece(chip_at(-sign * (r - 1)), core, h)
        return pltpu.make_async_remote_copy(
            src_ref=ref,
            dst_ref=ref,
            send_sem=ring_send.at[r - 1, way, h],
            recv_sem=ring_recv.at[r - 1, way, h],
            device_id={"dp": chip_at(sign) * 2 + core},
            device_id_type=MESH,
        )

    def sibling(r, way, h):
        sign = 1 if way == 0 else -1
        ref = piece(chip_at(-sign * r), core, h)
        return pltpu.make_async_remote_copy(
            src_ref=ref,
            dst_ref=ref,
            send_sem=sib_send.at[r, way, h],
            recv_sem=sib_recv.at[r, way, h],
            device_id={"dp": mz * 2 + 1 - core},
            device_id_type=MESH,
        )

    def ring_step(r):
        for way, h in hops(r):
            ring(r, way, h).wait_recv()
            if r < rounds and (way, h) in hops(r + 1):
                ring(r + 1, way, h).start()
            sibling(r, way, h).start()

    for way, h in hops(1):
        ring(1, way, h).start()
    for h in range(2):
        sibling(0, 0, h).start()
    EARLY(send_bands, chips, 2)

    scaled_xy = scaled_all[own_rows, :]
    scaled_yx = nn(swap, scaled_xy).astype(BF16)
    loads[4].wait()

    def back(hop, q):
        out, into = ((back_out1, back_in1), (back_out2, back_in2))[hop]
        return out.at[q], into.at[q], back_sems.at[4 * hop + q]

    for q in (0, 2, 1, 3):
        lhs = scaled_xy if q < 2 else scaled_yx
        back_out1[q] = nt(lhs, w[pl.ds(q * part, part), :]).astype(BF16)
        spread(*back(0, q), to_x=q < 2)

    def turn(q):
        spread_wait(*back(0, q)).wait_recv()
        back_out2[q] = nn(swap, back_in1[q]).astype(BF16)
        spread(*back(1, q), to_x=q >= 2)

    table_back = [nt(eye, table).astype(BF16) for table in (table_yx, table_xy)]

    def combine(q):
        spread_wait(*back(1, q)).wait_recv()
        input_grad[:, pl.ds(q * part, part)] = nn(table_back[q // 2], back_in2[q]).astype(BF16)

    def product(chip):
        at = pl.ds(pl.multiple_of(chip * 2 * slots, 2 * slots), 2 * slots)
        return nn(bands[chip], scaled_all[at, :])

    jobs = [[(turn, 0), (turn, 2)], [(turn, 1), (turn, 3)], [(combine, 0), (combine, 2)], [(combine, 1), (combine, 3)]]
    for r in range(1, max(rounds, 4) + 1):
        if r <= 4:
            for job, q in jobs[r - 1]:
                job(q)
        if r < rounds:
            ring_step(r)

    for j in range(3):
        band_wait(j).wait_recv()
    for h in range(2):
        sibling(0, 0, h).wait_recv()
    total[...] = product(mz)
    for r in range(1, rounds):
        for way, h in hops(r):
            sibling(r, way, h).wait_recv()
        total[...] += product(chip_at(-r))
        total[...] += product(chip_at(r))
    ring_step(rounds)
    for way, h in hops(rounds):
        sibling(rounds, way, h).wait_recv()
    weight_grad[...] = (total[...] + product(chip_at(rounds))).astype(BF16)

    for i in range(2):
        for hop in range(2):
            spread_wait(*rows(hop, i)).wait_send()
    for q in range(4):
        for hop in range(2):
            spread_wait(*back(hop, q)).wait_send()
    for j in range(3):
        band_wait(j).wait_send()
    for h in range(2):
        sibling(0, 0, h).wait_send()
    for r in range(1, rounds + 1):
        for way, h in hops(r):
            ring(r, way, h).wait_send()
            sibling(r, way, h).wait_send()


def EARLY(send_bands, chips, place):
    if place == 0:
        send_bands(0, chips)


def on_device(side, grad_out, routes, gates, weights, saved_inputs):
    replicas = lax.axis_size("dp")
    chips = replicas // 2
    slots, width = saved_inputs.shape[2:]
    tokens, ff = grad_out.shape
    half, part, band = ff // 2, width // 4, width // replicas
    rounds = chips // 2
    ids, gate_rows = routes.T, gates.T
    dma = pltpu.SemaphoreType.DMA
    scratch = [
        pltpu.VMEM(ids.shape, jnp.int32),
        pltpu.VMEM(gate_rows.shape, F32),
        pltpu.VMEM((tokens, ff), BF16),
        pltpu.VMEM((width, ff), BF16),
        pltpu.VMEM((slots, width), BF16),
        dma((5,)),
        *[pltpu.VMEM((2, slots, half), BF16)] * 4,
        dma((4, 2)),
        pltpu.VMEM((width, slots), BF16),
        pltpu.VMEM((chips, band, 2 * slots), BF16),
        dma((2, 3)),
        pltpu.VMEM((replicas * slots, ff), BF16),
        dma((rounds, 2, 2)),
        dma((rounds, 2, 2)),
        dma((rounds + 1, 2, 2)),
        dma((rounds + 1, 2, 2)),
        *[pltpu.VMEM((4, slots, part), BF16)] * 4,
        dma((8, 2)),
        pltpu.VMEM((band, ff), F32),
    ]
    input_grad, weight_grad = pl.pallas_call(
        functools.partial(kernel, side, chips),
        out_shape=(
            jax.ShapeDtypeStruct((tokens, width), BF16),
            jax.ShapeDtypeStruct((band, ff), BF16),
        ),
        in_specs=[pl.BlockSpec(memory_space=pl.ANY)] * 5,
        out_specs=[pl.BlockSpec(memory_space=pltpu.VMEM)] * 2,
        scratch_shapes=scratch,
        compiler_params=pltpu.CompilerParams(
            collective_id=0, has_side_effects=True, vmem_limit_bytes=48 << 20
        ),
    )(ids, gate_rows, grad_out, weights.reshape(width, ff), saved_inputs.reshape(slots, width))
    return input_grad, weight_grad[None]


def solution(mesh):
    side = int(round(mesh.shape["expert"] ** 0.5))
    return jax.shard_map(
        functools.partial(on_device, side),
        mesh=mesh,
        in_specs=(
            P(("dp", "expert"), None),
            P(("dp", "expert"), None),
            P(("dp", "expert"), None),
            P("expert", None, None),
            P("dp", "expert", None, None),
        ),
        out_specs=(P(("dp", "expert"), None), P("expert", "dp", None)),
        check_vma=False,
    )
```

time: 131 us -> 74.7 us (0.57)
  Pallas kernels: 0 us -> 68.7 us
  waiting for transfers between devices: 42.3 us -> 0 us
  starting transfers between devices: 30.6 us -> 0 us
  blocking collectives: 26.3 us -> 0 us
  between operations: 14.1 us -> 0.65 us
  matrix products: 11.7 us -> 0 us
    pallas_call x0 -> x1, Pallas kernels: none -> 68.7 us  [on_device(): pl.pallas_call(functools.partial(kernel, side, chips), out_shape=(jax.Sha...]
    all_to_all x2 -> x0, waiting for transfers between devices: 42.3 us -> none  [the longest x1 23.6 us: on_device(): lax.all_to_all(saved_rows, 'dp', split_axis=1, concat_axis=0, tiled=True)]
    all_to_all x2 -> x0, starting transfers between devices: 30.6 us -> none  [the longest x1 25.9 us: on_device(): lax.all_to_all(saved_rows, 'dp', split_axis=1, concat_axis=0, tiled=True)]
    all_to_all x1 -> x0, blocking collectives: 26.3 us -> none  [on_device(): lax.all_to_all(scaled_out.reshape(experts, capacity, ff), 'expert', split...]
    dot_general x5 -> x0, matrix products: 11.7 us -> none  [the longest x1 5.77 us: on_device(): lax.dot_general(scaled, weights[0], (((1,), (1,)), ((), ())), preferred_e...]
    unnamed x5 -> x10, local copies, waits for them, and re-layouts: 1.32 us -> 5.17 us
    reshape x4 -> x0, local copies, waits for them, and re-layouts: 2.51 us -> none  [the longest x1 1.27 us: on_device(): answers.reshape(experts, capacity, model_width)]
  transfers between devices with their start and end apart: 3 -> 0, of which waited for: 2 -> 0; matrix products, arithmetic and copies ran while one was open for 8% -> 0% of each run, Pallas kernels for 0% -> 0%
where the time goes in v2:
time: 74.7 us; the launch traced here: 74.5 us
  Pallas kernels  68.7 us (92%)
  local copies, waits for them, and re-layouts  5.17 us (7%)
    pallas_call x1, Pallas kernels, on_device(): pl.pallas_call(functools.partial(kernel, side, chips), out_shape=(jax.Sha...  68.7 us
    unnamed x10, local copies, waits for them, and re-layouts  5.17 us

profile of v2, /device:TPU:1, one launch (start us, length us, event | category | flops | bytes accessed | tf_op | source)
XLA Modules:
  0.0 74.5 jit_solution(11455850323905569636)
XLA Ops:
  0.6 0.0 copy-start
  0.6 1.2 %copy-done = bf16[1,1,128,3584]{3,2,1,0:T(8,128)(2,1)S(1)} copy-done((bf16[1,1,128,3584]{3,2,1,0:T(8,128)(2,1)S(1)}, bf16[1,1,128,3584]{3,2,1,0:T(8,128)(2,1)}, u32[]{:S(2)}) %copy-start) | copy-done | bytes 917528
  1.8 0.0 copy-start.1
  1.8 0.9 %copy-done.1 = bf16[128,1024]{1,0:T(8,128)(2,1)S(1)} copy-done((bf16[128,1024]{1,0:T(8,128)(2,1)S(1)}, bf16[128,1024]{1,0:T(8,128)(2,1)}, u32[]{:S(2)}) %copy-start.1) | copy-done | bytes 262168
  2.8 0.0 copy-start.2
  2.8 0.7 copy-done.2
  3.4 0.0 copy-start.3
  3.4 0.7 copy-done.3
  4.1 68.7 %shard_map.68 = (bf16[128,3584]{1,0:T(8,128)(2,1)S(1)}, bf16[224,1024]{1,0:T(8,128)(2,1)S(1)}) custom-call(s32[2,128]{1,0:T(2,128)S(1)} %bitcast.7, f32[2,128]{1,0:T(2,128)S(1)} %bitcast.8, bf16[128,1024]{1,0:T(8,128)(2,1)S(1)} %copy-done.1, bf16[3584,1024]{1,0:T(8,128)(2,1)} %bitcast.9, bf16[128,3584]{1,0:T(8,128)(2,1)S(1)} %bitcast.5), custom_call_target="tpu_custom_call" | custom-call | tf_op jit(solution)/shard_map/pallas_call | solution.py:334
  72.8 0.9 %copy.9 = bf16[128,3584]{1,0:T(8,128)(2,1)} copy(bf16[128,3584]{1,0:T(8,128)(2,1)S(1)} %get-tuple-element.8) | data formatting | bytes 1835008
  73.7 0.8 %copy.10 = bf16[1,224,1024]{2,1,0:T(8,128)(2,1)} copy(bf16[1,224,1024]{2,1,0:T(8,128)(2,1)S(1)} %bitcast.6) | data formatting | bytes 917504
Async XLA Ops:
  0.6 1.2 %copy-start = (bf16[1,1,128,3584]{3,2,1,0:T(8,128)(2,1)S(1)}, bf16[1,1,128,3584]{3,2,1,0:T(8,128)(2,1)}, u32[]{:S(2)}) copy-start(bf16[1,1,128,3584]{3,2,1,0:T(8,128)(2,1)} %param.9) | copy-start | bytes 2752516
  1.8 0.9 %copy-start.1 = (bf16[128,1024]{1,0:T(8,128)(2,1)S(1)}, bf16[128,1024]{1,0:T(8,128)(2,1)}, u32[]{:S(2)}) copy-start(bf16[128,1024]{1,0:T(8,128)(2,1)} %grad_hbm.1) | copy-start | bytes 786436
  2.8 0.7 copy-start.2
  3.4 0.7 copy-start.3

commit v3 on v2

--- a/solution.py
+++ b/solution.py
@@ -8,6 +8,7 @@
 from jax.sharding import PartitionSpec as P
 
 MESH = pl.DeviceIdType.MESH
+PIECES = 2
 BF16, F32 = jnp.bfloat16, jnp.float32
 
 
@@ -22,13 +23,13 @@
 def kernel(
     side, chips,
     ids_hbm, gates_hbm, grad_hbm, w_hbm, saved_hbm,
-    input_grad, weight_grad,
+    input_grad_hbm, weight_grad_hbm,
     ids, gates, grad, w, saved, local_sems,
     rows_out1, rows_in1, rows_out2, rows_in2, rows_sems,
     saved_t, bands, band_sems,
     scaled_all, ring_send, ring_recv, sib_send, sib_recv,
     back_out1, back_in1, back_out2, back_in2, back_sems,
-    total,
+    total, input_grad, weight_grad, store_sems,
 ):
     slots, width = saved.shape
     ff = grad.shape[1]
@@ -38,6 +39,7 @@
     band = bands.shape[1]
     bits = side.bit_length() - 1
     rounds = chips // 2
+    cut = ff // PIECES
     rep, spot = lax.axis_index("dp"), lax.axis_index("expert")
     mz, core = lax.div(rep, 2), lax.rem(rep, 2)
     mx, my = lax.div(spot, side), lax.rem(spot, side)
@@ -101,6 +103,10 @@
     loads[2].wait()
     rows_out1[0] = (nn(table_xy, grad[:, :half]) * gate_xy).astype(BF16)
     rows_out1[1] = (nn(table_yx, grad[:, half:]) * gate_yx).astype(BF16)
+
+    loads[3].wait()
+    for start in range(0, width, slots):
+        saved_t[pl.ds(start, slots), :] = nt(same, saved[:, start : start + slots]).astype(BF16)
 
     pl.semaphore_wait(barrier, 2 * (side - 1) + 2 * chips - 1)
 
@@ -137,10 +143,6 @@
     for i in range(2):
         spread(*rows(0, i), to_x=i == 0)
 
-    loads[3].wait()
-    for start in range(0, width, slots):
-        saved_t[pl.ds(start, slots), :] = nt(same, saved[:, start : start + slots]).astype(BF16)
-
     def send_bands(first, last):
         for k in range(first, last):
             for other in range(2):
@@ -168,7 +170,7 @@
             device_id_type=MESH,
         )
 
-    EARLY(send_bands, chips, 0)
+    send_bands(0, chips)
     bands[mz, :, pl.ds(pl.multiple_of(core * slots, slots), slots)] = saved_t[
         pl.ds(pl.multiple_of(rep * band, band), band), :
     ]
@@ -177,7 +179,6 @@
         spread_wait(*rows(0, i)).wait_recv()
         rows_out2[i] = nn(swap, rows_in1[i]).astype(BF16)
         spread(*rows(1, i), to_x=i == 1)
-    EARLY(send_bands, chips, 1)
     own_rows = pl.ds(pl.multiple_of(rep * slots, slots), slots)
     for i in range(2):
         spread_wait(*rows(1, i)).wait_recv()
@@ -186,11 +187,13 @@
 
     def piece(chip, which, h):
         return scaled_all.at[
-            pl.ds(pl.multiple_of((chip * 2 + which) * slots, slots), slots), pl.ds(h * half, half)
+            pl.ds(pl.multiple_of((chip * 2 + which) * slots, slots), slots), pl.ds(h * cut, cut)
         ]
 
     def hops(r):
-        return [(0, 0), (1, 0), (0, 1), (1, 1)] if r < rounds else [(0, 0), (1, 1)]
+        if r < rounds:
+            return [(way, h if way == 0 else PIECES - 1 - h) for h in range(PIECES) for way in range(2)]
+        return [(way, h if way == 0 else PIECES - 1 - h) for h in range(PIECES // 2) for way in range(2)]
 
     def ring(r, way, h):
         sign = 1 if way == 0 else -1
@@ -225,9 +228,8 @@
 
     for way, h in hops(1):
         ring(1, way, h).start()
-    for h in range(2):
+    for h in range(PIECES):
         sibling(0, 0, h).start()
-    EARLY(send_bands, chips, 2)
 
     scaled_xy = scaled_all[own_rows, :]
     scaled_yx = nn(swap, scaled_xy).astype(BF16)
@@ -249,36 +251,51 @@
 
     table_back = [nt(eye, table).astype(BF16) for table in (table_yx, table_xy)]
 
+    def store_part(q):
+        columns = pl.ds(q * part, part)
+        return pltpu.make_async_copy(
+            input_grad.at[:, columns], input_grad_hbm.at[:, columns], store_sems.at[q]
+        )
+
     def combine(q):
         spread_wait(*back(1, q)).wait_recv()
         input_grad[:, pl.ds(q * part, part)] = nn(table_back[q // 2], back_in2[q]).astype(BF16)
+        store_part(q).start()
 
     def product(chip):
         at = pl.ds(pl.multiple_of(chip * 2 * slots, 2 * slots), 2 * slots)
         return nn(bands[chip], scaled_all[at, :])
 
-    jobs = [[(turn, 0), (turn, 2)], [(turn, 1), (turn, 3)], [(combine, 0), (combine, 2)], [(combine, 1), (combine, 3)]]
-    for r in range(1, max(rounds, 4) + 1):
-        if r <= 4:
-            for job, q in jobs[r - 1]:
-                job(q)
-        if r < rounds:
-            ring_step(r)
-
-    for j in range(3):
-        band_wait(j).wait_recv()
-    for h in range(2):
-        sibling(0, 0, h).wait_recv()
-    total[...] = product(mz)
-    for r in range(1, rounds):
+    def add(r):
         for way, h in hops(r):
             sibling(r, way, h).wait_recv()
         total[...] += product(chip_at(-r))
         total[...] += product(chip_at(r))
+
+    jobs = [(turn, (0, 2)), (turn, (1, 3)), (combine, (0, 2)), (combine, (1, 3))]
+    for r in range(1, max(rounds, 4) + 1):
+        if r <= 4:
+            job, parts = jobs[r - 1]
+            for q in parts:
+                job(q)
+        if r < rounds:
+            ring_step(r)
+
+    for j in range(3):
+        band_wait(j).wait_recv()
+    for h in range(PIECES):
+        sibling(0, 0, h).wait_recv()
+    total[...] = product(mz)
+    for r in range(1, rounds - 1):
+        add(r)
     ring_step(rounds)
+    if rounds > 1:
+        add(rounds - 1)
     for way, h in hops(rounds):
         sibling(rounds, way, h).wait_recv()
     weight_grad[...] = (total[...] + product(chip_at(rounds))).astype(BF16)
+    store = pltpu.make_async_copy(weight_grad, weight_grad_hbm, store_sems.at[4])
+    store.start()
 
     for i in range(2):
         for hop in range(2):
@@ -288,17 +305,15 @@
             spread_wait(*back(hop, q)).wait_send()
     for j in range(3):
         band_wait(j).wait_send()
-    for h in range(2):
+    for q in range(4):
+        store_part(q).wait()
+    for h in range(PIECES):
         sibling(0, 0, h).wait_send()
     for r in range(1, rounds + 1):
         for way, h in hops(r):
             ring(r, way, h).wait_send()
             sibling(r, way, h).wait_send()
-
-
-def EARLY(send_bands, chips, place):
-    if place == 0:
-        send_bands(0, chips)
+    store.wait()
 
 
 def on_device(side, grad_out, routes, gates, weights, saved_inputs):
@@ -323,13 +338,16 @@
         pltpu.VMEM((chips, band, 2 * slots), BF16),
         dma((2, 3)),
         pltpu.VMEM((replicas * slots, ff), BF16),
-        dma((rounds, 2, 2)),
-        dma((rounds, 2, 2)),
-        dma((rounds + 1, 2, 2)),
-        dma((rounds + 1, 2, 2)),
+        dma((rounds, 2, PIECES)),
+        dma((rounds, 2, PIECES)),
+        dma((rounds + 1, 2, PIECES)),
+        dma((rounds + 1, 2, PIECES)),
         *[pltpu.VMEM((4, slots, part), BF16)] * 4,
         dma((8, 2)),
         pltpu.VMEM((band, ff), F32),
+        pltpu.VMEM((tokens, width), BF16),
+        pltpu.VMEM((band, ff), BF16),
+        dma((5,)),
     ]
     input_grad, weight_grad = pl.pallas_call(
         functools.partial(kernel, side, chips),
@@ -337,11 +355,11 @@
             jax.ShapeDtypeStruct((tokens, width), BF16),
             jax.ShapeDtypeStruct((band, ff), BF16),
         ),
-        in_specs=[pl.BlockSpec(memory_space=pl.ANY)] * 5,
-        out_specs=[pl.BlockSpec(memory_space=pltpu.VMEM)] * 2,
+        in_specs=[pl.BlockSpec(memory_space=pltpu.HBM)] * 5,
+        out_specs=[pl.BlockSpec(memory_space=pltpu.HBM)] * 2,
         scratch_shapes=scratch,
         compiler_params=pltpu.CompilerParams(
-            collective_id=0, has_side_effects=True, vmem_limit_bytes=48 << 20
+            collective_id=0, has_side_effects=True, vmem_limit_bytes=61_000_000
         ),
     )(ids, gate_rows, grad_out, weights.reshape(width, ff), saved_inputs.reshape(slots, width))
     return input_grad, weight_grad[None]

time: 74.7 us -> 71.9 us (0.963)
  Pallas kernels: 68.7 us -> 67 us
  local copies, waits for them, and re-layouts: 5.17 us -> 3.98 us
    pallas_call x1, Pallas kernels: 68.7 us -> 67 us  [on_device(): pl.pallas_call(functools.partial(kernel, side, chips), out_shape=(jax.Sha...]
    unnamed x10 -> x2, local copies, waits for them, and re-layouts: 5.17 us -> 3.98 us
where the time goes in v3:
time: 71.9 us; the launch traced here: 71.6 us
  Pallas kernels  67 us (93%)
  local copies, waits for them, and re-layouts  3.98 us (6%)
    pallas_call x1, Pallas kernels, on_device(): pl.pallas_call(functools.partial(kernel, side, chips), out_shape=(jax.Sha...  67 us
    unnamed x2, local copies, waits for them, and re-layouts  3.98 us

profile of v3, /device:TPU:1, one launch (start us, length us, event | category | flops | bytes accessed | tf_op | source)
XLA Modules:
  0.0 71.6 jit_solution(16147969276835522143)
XLA Ops:
  0.6 67.0 %shard_map.68 = (bf16[128,3584]{1,0:T(8,128)(2,1)}, bf16[224,1024]{1,0:T(8,128)(2,1)}) custom-call(s32[2,128]{1,0:T(2,128)} %bitcast.8, f32[2,128]{1,0:T(2,128)} %bitcast.9, bf16[128,1024]{1,0:T(8,128)(2,1)} %grad_hbm.1, bf16[3584,1024]{1,0:T(8,128)(2,1)} %bitcast.5, bf16[128,3584]{1,0:T(8,128)(2,1)} %bitcast.6), custom_call_target="tpu_custom_call" | custom-call | tf_op jit(solution)/shard_map/pallas_call | solution.py:352
  67.7 2.2 %copy.9 = bf16[128,3584]{1,0:T(8,128)(2,1)} copy(bf16[128,3584]{1,0:T(8,128)(2,1)} %get-tuple-element.8) | data formatting | bytes 1835008
  69.8 1.8 %copy.10 = bf16[1,224,1024]{2,1,0:T(8,128)(2,1)} copy(bf16[1,224,1024]{2,1,0:T(8,128)(2,1)} %bitcast.7) | data formatting | bytes 917504
